TPU v7x, 256 devices: a whole 4x4x8 slice. The times are simulated.
256 devices in a mesh: section: 16 (over x, z_lo), expert: 16 (over y, z_hi, core).
Axes of the slice: x: 4, y: 4, z: 8 (z_hi: 2, z_lo: 4; z = z_hi * 4 + z_lo), core: 2. Of those that a mesh axis runs over, the one named last changes fastest.
Arguments:
- fwd_tokens: bfloat16 [16, 2048, 2048], P('section', 'expert'), may hold values from -6 to 6
- fwd_experts: int32 [16, 2048, 8], P('section', 'expert'), may hold values from 0 to 15, all different within a row; in each aligned block of 128 rows (0 to 127, 128 to 255, ..., all dimensions but the last counted through in order) at most 80 rows name the same one
- fwd_gates: float32 [16, 2048, 8], P('section', 'expert'), may hold values from 0.1 to 0.5
- gate_proj: bfloat16 [16, 16, 2048, 384], P('section', 'expert'), may hold values from -0.125 to 0.125
- up_proj: bfloat16 [16, 16, 2048, 384], P('section', 'expert'), may hold values from -0.125 to 0.125
- down_proj: bfloat16 [16, 16, 384, 2048], P('section', 'expert'), may hold values from -0.3125 to 0.3125
- bwd_grads: bfloat16 [16, 2048, 2048], P('section', 'expert'), may hold values from -6 to 6
- bwd_experts: int32 [16, 2048, 8], P('section', 'expert'), may hold values from 0 to 15, all different within a row; in each aligned block of 128 rows (0 to 127, 128 to 255, ..., all dimensions but the last counted through in order) at most 80 rows name the same one
- bwd_gates: float32 [16, 2048, 8], P('section', 'expert'), may hold values from 0.1 to 0.5
- saved_pre: bfloat16 [16, 16, 16, 80, 768], P('section', None, 'expert'), may hold values from -6 to 6
Outputs:
- fwd_next: bfloat16 [16, 2048, 2048], P('section', 'expert')
- grad_prev: bfloat16 [16, 2048, 2048], P('section', 'expert')
Inputs may be any that keep to these rules, and one draw needn't show every extreme that they name: `fwd_experts`: each token names 8 different experts; within a section, the 128 tokens of one index of expert name no expert more than 80 times, a bound that some block reaches. `bwd_experts`: as for fwd_experts.
All inputs are finite; a program needn't handle non-finite values.
Results may differ from a plain program's by a relative error of at most 0.0053.
Values may be sent and summed in bfloat16 or wider, within the bound.
A program may use at most 128 MiB of HBM per device.

v0:
```python
import jax
import jax.numpy as jnp
from jax import lax
from jax.sharding import PartitionSpec as P


def from_behind(shard, axis, by):
    count = lax.axis_size(axis)
    return lax.ppermute(shard, axis, [(i, (i + by) % count) for i in range(count)])


def slot_tables(expert_ids, experts_all, capacity):
    token_count, choice_count = expert_ids.shape
    onehot = jnp.sum(
        (expert_ids[:, :, None] == jnp.arange(experts_all, dtype=jnp.int32)[None, None, :]).astype(
            jnp.int32
        ),
        axis=1,
    )
    ahead = jnp.cumsum(onehot, axis=0) - onehot
    place = jnp.take_along_axis(ahead, expert_ids, axis=1)
    slot_rows = expert_ids * capacity + place
    flat_rows = slot_rows.reshape(-1)
    owner = (
        jnp.zeros((experts_all * capacity,), jnp.int32)
        .at[flat_rows]
        .set(jnp.arange(token_count * choice_count, dtype=jnp.int32))
    )
    filled = jnp.zeros((experts_all * capacity,), jnp.bool_).at[flat_rows].set(True)
    return (slot_rows, owner, filled)


def shards(
    fwd_tokens,
    fwd_experts,
    fwd_gates,
    gate_proj,
    up_proj,
    down_proj,
    bwd_grads,
    bwd_experts,
    bwd_gates,
    saved_pre,
):
    width = fwd_tokens.shape[2]
    hidden_units = gate_proj.shape[3]
    local_experts = gate_proj.shape[1]
    peers = lax.axis_size("expert")
    experts_all = peers * local_experts
    capacity = saved_pre.shape[3]
    target_shape = (peers, local_experts, capacity, width)
    w_gate = gate_proj[0]
    w_up = up_proj[0]
    w_down = down_proj[0]
    inputs = fwd_tokens[0]
    grads = bwd_grads[0]
    choice_count = fwd_experts.shape[2]
    fwd_slot, fwd_owner, fwd_filled = slot_tables(fwd_experts[0], experts_all, capacity)
    fwd_rows = jnp.where(
        fwd_filled[:, None], inputs[fwd_owner // choice_count], jnp.zeros((), inputs.dtype)
    )
    fwd_buffer = fwd_rows.reshape(target_shape)
    bwd_slot, bwd_owner, bwd_filled = slot_tables(bwd_experts[0], experts_all, capacity)
    slot_gate = jnp.where(
        bwd_filled, bwd_gates[0].reshape(-1)[bwd_owner], jnp.zeros((), jnp.float32)
    )
    bwd_rows = (slot_gate[:, None] * grads[bwd_owner // choice_count].astype(jnp.float32)).astype(
        jnp.bfloat16
    )
    bwd_buffer = bwd_rows.reshape(target_shape)
    saved_local = saved_pre[0]
    received = lax.all_to_all(fwd_buffer, "expert", split_axis=0, concat_axis=0, tiled=True)
    gate_act = jnp.einsum("nscd,sdf->nscf", received, w_gate, preferred_element_type=jnp.float32)
    up_act = jnp.einsum("nscd,sdf->nscf", received, w_up, preferred_element_type=jnp.float32)
    hidden = (jax.nn.silu(gate_act) * up_act).astype(jnp.bfloat16)
    fwd_results = jnp.einsum(
        "nscf,sfd->nscd", hidden, w_down, preferred_element_type=jnp.float32
    ).astype(jnp.bfloat16)
    bwd_received = lax.all_to_all(bwd_buffer, "expert", split_axis=0, concat_axis=0, tiled=True)
    grad_hidden = jnp.einsum(
        "nscd,sfd->nscf", bwd_received, w_down, preferred_element_type=jnp.float32
    )
    pre_gate = saved_local[..., :hidden_units].astype(jnp.float32)
    pre_up = saved_local[..., hidden_units:].astype(jnp.float32)
    sigma = jax.nn.sigmoid(pre_gate)
    grad_gate = (grad_hidden * pre_up * sigma * (1.0 + pre_gate * (1.0 - sigma))).astype(
        jnp.bfloat16
    )
    grad_up = (grad_hidden * pre_gate * sigma).astype(jnp.bfloat16)
    grad_slot = jnp.einsum("nscf,sdf->nscd", grad_gate, w_gate, preferred_element_type=jnp.float32)
    grad_slot = grad_slot + jnp.einsum(
        "nscf,sdf->nscd", grad_up, w_up, preferred_element_type=jnp.float32
    )
    bwd_results = grad_slot.astype(jnp.bfloat16)
    fwd_returned = lax.all_to_all(fwd_results, "expert", split_axis=0, concat_axis=0, tiled=True)
    bwd_returned = lax.all_to_all(bwd_results, "expert", split_axis=0, concat_axis=0, tiled=True)
    fwd_picked = fwd_returned.reshape(-1, width)[fwd_slot]
    weighted = jnp.sum(fwd_gates[0][:, :, None] * fwd_picked.astype(jnp.float32), axis=1)
    mixed = (inputs.astype(jnp.float32) + weighted).astype(jnp.bfloat16)
    bwd_picked = bwd_returned.reshape(-1, width)[bwd_slot]
    grad_tokens = (
        grads.astype(jnp.float32) + jnp.sum(bwd_picked.astype(jnp.float32), axis=1)
    ).astype(jnp.bfloat16)
    fwd_next = from_behind(mixed[None], "section", 1)
    grad_prev = from_behind(grad_tokens[None], "section", -1)
    return (fwd_next, grad_prev)


def solution(mesh):
    placed = (
        P("section", "expert", None),
        P("section", "expert", None),
        P("section", "expert", None),
        P("section", "expert", None, None),
        P("section", "expert", None, None),
        P("section", "expert", None, None),
        P("section", "expert", None),
        P("section", "expert", None),
        P("section", "expert", None),
        P("section", None, "expert", None, None),
    )
    return jax.shard_map(
        shards,
        mesh=mesh,
        in_specs=placed,
        out_specs=(P("section", "expert", None), P("section", "expert", None)),
        check_vma=False,
    )
```

profile of v0, /device:TPU:96, one launch (start us, length us, event | category | flops | bytes accessed | tf_op | source)
XLA Modules:
  0.0 580.5 jit_solution(18283088039889658262)
XLA Ops:
  2.7 7.1 %gather_fusion.6 = s32[1024]{0:T(1024)S(1)} fusion(s32[128,16]{1,0:T(8,128)S(1)} %sub.21, s32[1024]{0:T(1024)S(1)} %reshape.297), kind=kCustom, calls=%fused_computation.1.clone | custom fusion | bytes 16384 | tf_op jit(solution)/shard_map/jit(take_along_axis)/gather | solution.py:21
  14.6 5.0 gather_fusion.2
  24.0 6.1 %gather_fusion.3 = bf16[1280,2048]{1,0:T(8,128)(2,1)} fusion(bf16[128,2048]{1,0:T(8,128)(2,1)S(1)} %bitcast.175, s32[2048]{0:T(1024)S(1)} %get-tuple-element.9), kind=kCustom, calls=%fused_computation.5 | custom fusion | bytes 10490880 | tf_op jit(solution)/shard_map/gather | solution.py:67
  30.1 5.8 fusion
  35.9 9.2 %all-to-all-start.2 = ((bf16[16,1,80,2048]{3,2,1,0:T(8,128)(2,1)}), bf16[16,1,80,2048]{3,2,1,0:T(8,128)(2,1)}, u32[]{:S(2)}, u32[]{:S(2)}) async-start(bf16[16,1,80,2048]{3,2,1,0:T(8,128)(2,1)} %fusion), calls=%async_computation.2 | async-start | bytes 10485760 | tf_op jit(solution)/shard_map/all_to_all | solution.py:79
  45.6 7.1 %gather_fusion.5 = s32[1024]{0:T(1024)S(1)} fusion(s32[128,16]{1,0:T(8,128)S(1)} %sub.19, s32[1024]{0:T(1024)S(1)} %reshape.292), kind=kCustom, calls=%fused_computation.clone | custom fusion | bytes 16384 | tf_op jit(solution)/shard_map/jit(take_along_axis)/gather | solution.py:21
  61.7 6.2 %gather_fusion = bf16[1280,2048]{1,0:T(8,128)(2,1)} fusion(bf16[128,2048]{1,0:T(8,128)(2,1)S(1)} %bitcast.176, s32[2048]{0:T(1024)S(1)} %pad_clamp_fusion.2), kind=kCustom, calls=%fused_computation.2 | custom fusion | bytes 10490880 | tf_op jit(solution)/shard_map/gather | solution.py:60
  67.9 5.3 broadcast_select_fusion
  73.2 93.4 %all-to-all-done.2 = bf16[16,1,80,2048]{3,2,1,0:T(8,128)(2,1)} async-done(((bf16[16,1,80,2048]{3,2,1,0:T(8,128)(2,1)}), bf16[16,1,80,2048]{3,2,1,0:T(8,128)(2,1)}, u32[]{:S(2)}, u32[]{:S(2)}) %all-to-all-start.2) | async-done | bytes 5242912 | tf_op jit(solution)/shard_map/all_to_all | solution.py:79
  166.6 4.8 all-to-all-start
  171.4 5.4 fusion.3
  180.0 4.8 fusion.2
  184.9 108.1 %all-to-all-done = bf16[16,1,80,2048]{3,2,1,0:T(8,128)(2,1)} async-done(((bf16[16,1,80,2048]{3,2,1,0:T(8,128)(2,1)}), bf16[16,1,80,2048]{3,2,1,0:T(8,128)(2,1)}, u32[]{:S(2)}, u32[]{:S(2)}) %all-to-all-start) | async-done | bytes 5242912 | tf_op jit(solution)/shard_map/all_to_all | solution.py:72
  293.0 4.6 all-to-all-start.3
  297.6 7.2 %fusion.7 = f32[16,80,384]{2,1,0:T(8,128)} fusion(bf16[16,1,80,2048]{3,2,1,0:T(8,128)(2,1)} %all-to-all-done, bf16[1,1,2048,384]{3,2,1,0:T(8,128)(2,1)} %param.15), kind=kOutput, calls=%fused_computation.22 | convolution fusion | flops 2013265920 | bytes 8781824 | tf_op jit(solution)/shard_map/nscd,sdf->nscf/dot_general | solution.py:73
  304.7 9.9 %convert_bitcast_fusion = bf16[16,1,80,2048]{3,2,1,0:T(8,128)(2,1)} fusion(bf16[1,1,384,2048]{3,2,1,0:T(8,128)(2,1)} %param.17, bf16[1,1,2048,384]{3,2,1,0:T(8,128)(2,1)S(1)} %copy-done, bf16[16,1,80,2048]{3,2,1,0:T(8,128)(2,1)} %all-to-all-done, f32[16,80,384]{2,1,0:T(8,128)} %fusion.7), kind=kOutput, calls=%fused_computation.24 | convolution fusion | flops 4032102400 | bytes 15597568 | tf_op jit(solution)/shard_map/nscf,sfd->nscd/dot_general | solution.py:76
  314.6 104.9 %all-to-all-done.3 = bf16[16,1,80,2048]{3,2,1,0:T(8,128)(2,1)} async-done(((bf16[16,1,80,2048]{3,2,1,0:T(8,128)(2,1)}), bf16[16,1,80,2048]{3,2,1,0:T(8,128)(2,1)}, u32[]{:S(2)}, u32[]{:S(2)}) %all-to-all-start.3) | async-done | bytes 5242912 | tf_op jit(solution)/shard_map/all_to_all | solution.py:96
  419.4 4.8 all-to-all-start.1
  424.6 12.0 %gather_fusion.4 = bf16[1024,2048]{1,0:T(8,128)(2,1)} fusion(bf16[1280,2048]{1,0:T(8,128)(2,1)} %bitcast.54, s32[1024]{0:T(1024)S(1)} %broadcast_clamp_fusion), kind=kCustom, calls=%fused_computation.6 | custom fusion | bytes 8392704 | tf_op jit(solution)/shard_map/gather | solution.py:100
  436.6 5.1 convert_reduce_fusion
  441.8 104.9 %all-to-all-done.1 = bf16[16,1,80,2048]{3,2,1,0:T(8,128)(2,1)} async-done(((bf16[16,1,80,2048]{3,2,1,0:T(8,128)(2,1)}), bf16[16,1,80,2048]{3,2,1,0:T(8,128)(2,1)}, u32[]{:S(2)}, u32[]{:S(2)}) %all-to-all-start.1) | async-done | bytes 5242912 | tf_op jit(solution)/shard_map/all_to_all | solution.py:95
  546.8 12.0 %gather_fusion.1 = bf16[1024,2048]{1,0:T(8,128)(2,1)} fusion(bf16[1280,2048]{1,0:T(8,128)(2,1)} %bitcast.28, s32[1024]{0:T(1024)S(1)} %broadcast_clamp_fusion.1), kind=kCustom, calls=%fused_computation.3 | custom fusion | bytes 8392704 | tf_op jit(solution)/shard_map/gather | solution.py:97
  558.8 6.5 %fusion.1 = f32[128,2048]{1,0:T(8,128)S(1)} fusion(bf16[1024,2048]{1,0:T(8,128)(2,1)} %gather_fusion.1, f32[128,8]{1,0:T(8,128)S(1)} %copy.27), kind=kLoop, calls=%fused_computation.16 | loop fusion | flops 6029312 | bytes 5246976 | tf_op jit(solution)/shard_map/reduce_sum | solution.py:98
  565.5 13.2 %collective-permute-done = bf16[1,128,2048]{2,1,0:T(8,128)(2,1)S(1)} collective-permute-done((bf16[1,128,2048]{2,1,0:T(8,128)(2,1)S(1)}, bf16[1,128,2048]{2,1,0:T(8,128)(2,1)S(1)}, u32[]{:S(2)}, u32[]{:S(2)}) %collective-permute-start) | collective-permute-done | bytes 524320 | tf_op jit(solution)/shard_map/ppermute | solution.py:9
  (67 shorter events, 26.2 us)
Async XLA Ops:
  0.6 179.4 %copy-start = (bf16[1,1,2048,384]{3,2,1,0:T(8,128)(2,1)S(1)}, bf16[1,1,2048,384]{3,2,1,0:T(8,128)(2,1)}, u32[]{:S(2)}) copy-start(bf16[1,1,2048,384]{3,2,1,0:T(8,128)(2,1)} %param.16) | copy-start | bytes 4718596
  2.7 11.7 %copy-start.5 = (f32[1,128,8]{1,2,0:T(8,128)S(1)}, f32[1,128,8]{1,2,0:T(8,128)}, u32[]{:S(2)}) copy-start(f32[1,128,8]{1,2,0:T(8,128)} %param.20) | copy-start | bytes 12292
  14.6 9.4 %copy-start.1 = (bf16[1,128,2048]{2,1,0:T(8,128)(2,1)S(1)}, bf16[1,128,2048]{2,1,0:T(8,128)(2,1)}, u32[]{:S(2)}) copy-start(bf16[1,128,2048]{2,1,0:T(8,128)(2,1)} %param.18) | copy-start | bytes 1572868
  35.9 9.2 %copy-start.4 = (s32[1,128,8]{1,2,0:T(8,128)S(1)}, s32[1,128,8]{1,2,0:T(8,128)}, u32[]{:S(2)}) copy-start(s32[1,128,8]{1,2,0:T(8,128)} %param.13) | copy-start | bytes 12292
  35.9 130.7 %all-to-all-start.2 = ((bf16[16,1,80,2048]{3,2,1,0:T(8,128)(2,1)}), bf16[16,1,80,2048]{3,2,1,0:T(8,128)(2,1)}, u32[]{:S(2)}, u32[]{:S(2)}) async-start(bf16[16,1,80,2048]{3,2,1,0:T(8,128)(2,1)} %fusion), calls=%async_computation.2 | async-start | bytes 10485760 | tf_op jit(solution)/shard_map/all_to_all | solution.py:79
  45.6 16.1 %copy-start.2 = (bf16[1,128,2048]{2,1,0:T(8,128)(2,1)S(1)}, bf16[1,128,2048]{2,1,0:T(8,128)(2,1)}, u32[]{:S(2)}) copy-start(bf16[1,128,2048]{2,1,0:T(8,128)(2,1)} %param.12) | copy-start | bytes 1572868
  166.6 126.4 %all-to-all-start = ((bf16[16,1,80,2048]{3,2,1,0:T(8,128)(2,1)}), bf16[16,1,80,2048]{3,2,1,0:T(8,128)(2,1)}, u32[]{:S(2)}, u32[]{:S(2)}) async-start(bf16[16,1,80,2048]{3,2,1,0:T(8,128)(2,1)} %broadcast_select_fusion), calls=%async_computation | async-start | bytes 10485760 | tf_op jit(solution)/shard_map/all_to_all | solution.py:72
  171.4 5.5 copy-start.3
  171.4 5.5 copy-start.7
  293.0 126.4 %all-to-all-start.3 = ((bf16[16,1,80,2048]{3,2,1,0:T(8,128)(2,1)}), bf16[16,1,80,2048]{3,2,1,0:T(8,128)(2,1)}, u32[]{:S(2)}, u32[]{:S(2)}) async-start(bf16[16,1,80,2048]{3,2,1,0:T(8,128)(2,1)} %fusion.2), calls=%async_computation.3 | async-start | bytes 10485760 | tf_op jit(solution)/shard_map/all_to_all | solution.py:96
  314.6 109.9 %copy-start.6 = (f32[1,128,8]{1,2,0:T(8,128)S(1)}, f32[1,128,8]{1,2,0:T(8,128)}, u32[]{:S(2)}) copy-start(f32[1,128,8]{1,2,0:T(8,128)} %param.14) | copy-start | bytes 12292
  419.4 127.3 %all-to-all-start.1 = ((bf16[16,1,80,2048]{3,2,1,0:T(8,128)(2,1)}), bf16[16,1,80,2048]{3,2,1,0:T(8,128)(2,1)}, u32[]{:S(2)}, u32[]{:S(2)}) async-start(bf16[16,1,80,2048]{3,2,1,0:T(8,128)(2,1)} %convert_bitcast_fusion), calls=%async_computation.1 | async-start | bytes 10485760 | tf_op jit(solution)/shard_map/all_to_all | solution.py:95
  441.8 123.8 %collective-permute-start.1 = (bf16[1,128,2048]{2,1,0:T(8,128)(2,1)S(1)}, bf16[1,128,2048]{2,1,0:T(8,128)(2,1)S(1)}, u32[]{:S(2)}, u32[]{:S(2)}) collective-permute-start(bf16[1,128,2048]{2,1,0:T(8,128)(2,1)S(1)} %fusion.40), channel_id=1, source_target_pairs={{0,240},{16,0},{32,16},{48,32},{64,48},{80,64},{96,80},{112,96},{1... | collective-permute-start | bytes 1572872 | tf_op jit(solution)/shard_map/ppermute | solution.py:9
  565.4 13.3 %collective-permute-start = (bf16[1,128,2048]{2,1,0:T(8,128)(2,1)S(1)}, bf16[1,128,2048]{2,1,0:T(8,128)(2,1)S(1)}, u32[]{:S(2)}, u32[]{:S(2)}) collective-permute-start(bf16[1,128,2048]{2,1,0:T(8,128)(2,1)S(1)} %fusion.41), channel_id=1, source_target_pairs={{0,16},{16,32},{32,48},{48,64},{64,80},{80,96},{96,112},{112,128},... | collective-permute-start | bytes 1572872 | tf_op jit(solution)/shard_map/ppermute | solution.py:9
where the time goes:
time: 592 us; the launch traced here: 580 us
  waiting for transfers between devices  424 us (72%)
  local copies, waits for them, and re-layouts  76.7 us (13%)
  matrix products  30.4 us (5%)
  other arithmetic  24.1 us (4%)
  starting transfers between devices  23.5 us (4%)
    all_to_all x1, waiting for transfers between devices, shards(): lax.all_to_all(fwd_buffer, 'expert', split_axis=0, concat_axis=0, tiled=T...  108 us
    all_to_all x1, waiting for transfers between devices, shards(): lax.all_to_all(fwd_results, 'expert', split_axis=0, concat_axis=0, tiled=...  105 us
    all_to_all x1, waiting for transfers between devices, shards(): lax.all_to_all(bwd_results, 'expert', split_axis=0, concat_axis=0, tiled=...  105 us
    all_to_all x1, waiting for transfers between devices, shards(): lax.all_to_all(bwd_buffer, 'expert', split_axis=0, concat_axis=0, tiled=T...  93.4 us
    gather x6, local copies, waits for them, and re-layouts, slot_tables(): place = jnp.take_along_axis(ahead, expert_ids, axis=1)  14.5 us
    ppermute x2, waiting for transfers between devices, from_behind(): lax.ppermute(shard, axis, [(i, (i + by) % count) for i in range(count)])  13.2 us
    gather x1, local copies, waits for them, and re-layouts, shards(): bwd_picked = bwd_returned.reshape(-1, width)[bwd_slot]  12 us
    gather x1, local copies, waits for them, and re-layouts, shards(): fwd_picked = fwd_returned.reshape(-1, width)[fwd_slot]  12 us
  transfers between devices with their start and end apart: 6, of which 5 were waited for; matrix products, arithmetic and copies ran while one was open for 16% of the time, Pallas kernels for 0%

commit v1 on v0

v1 whole, which is shorter than its diff:
```python
import jax
import jax.numpy as jnp
from jax import lax
from jax.experimental import pallas as pl
from jax.experimental.pallas import tpu as pltpu
from jax.sharding import PartitionSpec as P

Y_SIZE, HALVES, CORES = 4, 2, 2
PIECE = 32
MESH = pl.DeviceIdType.MESH
F32, BF16 = jnp.float32, jnp.bfloat16


def dot(a, b):
    return lax.dot_general(a, b, (((1,), (0,)), ((), ())), preferred_element_type=F32)


def dot_t(a, b):
    return lax.dot_general(a, b, (((1,), (1,)), ((), ())), preferred_element_type=F32)


def body(
    tab_in, xf, xb, wg, wu, wd, saved, out_f, out_b,
    tok, tab, wgu, wdn, sav, xs, ys, act, hid, sel, sel_t, sgate, chosen, part, opp, near, rel,
    dma_send, dma_recv, dma_local,
):
    section, expert = lax.axis_index("section"), lax.axis_index("expert")
    sections = lax.axis_size("section")
    y, h, c = expert // (HALVES * CORES), (expert // CORES) % HALVES, expert % CORES
    rows, width = xf.shape
    units = wg.shape[1]
    cap = saved.shape[1]
    half = rows // 2
    lanes = 512

    def at(dy, dh=0, dc=0, ds=0):
        return (
            (section + ds + sections) % sections,
            (((y + dy + Y_SIZE) % Y_SIZE) * HALVES + (h + dh) % HALVES) * CORES + (c + dc) % CORES,
        )

    up, down, across, twin = at(1), at(-1), at(0, 1), at(0, 0, 1)
    nexts = (at(0, 0, 0, 1), at(0, 1, 0, 1))
    prevs = (at(0, 0, 0, -1), at(0, 1, 0, -1))

    count = [0, 0]
    remote = []

    def send(src, dst, device):
        i = count[0]
        count[0] += 1
        copy = pltpu.make_async_remote_copy(
            src_ref=src, dst_ref=dst, send_sem=dma_send.at[i], recv_sem=dma_recv.at[i],
            device_id=device, device_id_type=MESH,
        )
        remote.append(copy)
        return copy

    def local(src, dst):
        i = count[1]
        count[1] += 1
        return pltpu.make_async_copy(src, dst, dma_local.at[i])

    barrier = pltpu.get_barrier_semaphore()
    greeted = (up, down, across, twin) + nexts + prevs
    for device in greeted:
        pl.semaphore_signal(barrier, inc=1, device_id=device, device_id_type=MESH)

    inputs = (xf, xb)
    load_tok = [local(inputs[d], tok.at[d, 0]) for d in range(2)]
    load_w = [
        local(wg, wgu.at[0, :, pl.ds(0, units)]),
        local(wu, wgu.at[0, :, pl.ds(units, units)]),
        local(wd, wdn.at[0]),
    ]

    def block_of(j, core):
        hh, dy = j // Y_SIZE, j % Y_SIZE
        return (((y + dy) % Y_SIZE) * HALVES + (h + hh) % HALVES) * CORES + core

    load_s = [local(saved.at[block_of(j, c)], sav.at[0, j]) for j in range(8)]
    for copy in load_tok + load_w + load_s:
        copy.start()
    tab[0] = tab_in[...]
    pl.semaphore_wait(barrier, len(greeted))

    low, high = pl.ds(0, half), pl.ds(half, half)
    tab_z = send(tab.at[0], tab.at[4], across)
    tab_y = [(send(tab.at[4 * g], tab.at[4 * g + 3], up), send(tab.at[4 * g], tab.at[4 * g + 1], down)) for g in range(2)]
    tab_o = [send(tab.at[4 * g + 3], tab.at[4 * g + 2], up) for g in range(2)]

    def source(d, g, part_rows):
        return inputs[d].at[part_rows] if g == 0 else tok.at[d, 4, part_rows]

    own = {}
    fwd = {}
    over = {}
    for d in range(2):
        for i, r in enumerate((low, high)):
            over[d, i] = send(inputs[d].at[r], tok.at[d, 4, r], across)
        for g in range(2):
            for i, r in enumerate((low, high)):
                own[d, g, 0, i] = send(source(d, g, r), tok.at[d, 4 * g + 3, r], up)
                own[d, g, 1, i] = send(source(d, g, r), tok.at[d, 4 * g + 1, r], down)
            fwd[d, g, 0] = send(tok.at[d, 4 * g + 3, low], tok.at[d, 4 * g + 2, low], up)
            fwd[d, g, 1] = send(tok.at[d, 4 * g + 1, high], tok.at[d, 4 * g + 2, high], down)
    twin_w = [
        send(wg, wgu.at[1, :, pl.ds(0, units)], twin),
        send(wu, wgu.at[1, :, pl.ds(units, units)], twin),
        send(wd, wdn.at[1], twin),
    ]
    twin_s = [send(saved.at[block_of(j, 1 - c)], sav.at[1, j], twin) for j in range(8)]

    def start_own(d, g, i):
        own[d, g, 0, i].start()
        own[d, g, 1, i].start()

    def forward(d, g):
        own[d, g, 0, 0].wait_recv()
        fwd[d, g, 0].start()
        own[d, g, 1, 1].wait_recv()
        fwd[d, g, 1].start()

    def complete(d, g):
        own[d, g, 0, 1].wait_recv()
        own[d, g, 1, 0].wait_recv()
        fwd[d, g, 0].wait_recv()
        fwd[d, g, 1].wait_recv()

    experts = [(y * HALVES + h) * CORES + c, (y * HALVES + h) * CORES + (1 - c)]

    def select(d, g):
        for j in range(4):
            names = tab[4 * g + j, 16 * d : 16 * d + 8, :]
            gates = tab[4 * g + j, 16 * d + 8 : 16 * d + 16, :]
            for m in range(2):
                hit = names == experts[m].astype(F32)
                chosen[2 * j + m : 2 * j + m + 1, :] = jnp.sum(jnp.where(hit, 1.0, 0.0), axis=0, keepdims=True)
                chosen[8 + 2 * j + m : 9 + 2 * j + m, :] = jnp.sum(jnp.where(hit, gates, 0.0), axis=0, keepdims=True)
        earlier = lax.broadcasted_iota(jnp.int32, (rows, rows), 0) < lax.broadcasted_iota(jnp.int32, (rows, rows), 1)
        ahead = dot(chosen[0:8, :].astype(BF16), jnp.where(earlier, 1.0, 0.0).astype(BF16))
        place = lax.broadcasted_iota(jnp.int32, (cap, rows), 0).astype(F32)
        for j in range(4):
            for m in range(2):
                i = 2 * j + m
                taken = (place == ahead[i : i + 1, :]) & (chosen[i : i + 1, :] > 0.5)
                one = jnp.where(taken, 1.0, 0.0)
                sel[j, m * cap : (m + 1) * cap, :] = one
                sgate[j, m] = jnp.sum(one * chosen[8 + i : 9 + i, :], axis=1, keepdims=True)
            sel_t[j] = jnp.transpose(sel[j]).astype(BF16)

    def dispatch(d, g):
        for j in range(4):
            one = sel[j].astype(BF16)

            @pl.loop(0, width // lanes)
            def _(n):
                at_n = pl.ds(pl.multiple_of(n * lanes, lanes), lanes)
                moved = dot(one, tok[d, 4 * g + j, :, at_n]).reshape(2, cap, lanes)
                if d == 1:
                    moved = moved * sgate[j]
                xs[j, :, :, at_n] = moved.astype(BF16)

    def collect(d, g):
        for j in range(4):
            one = sel_t[j]

            @pl.loop(0, width // lanes)
            def _(n):
                at_n = pl.ds(pl.multiple_of(n * lanes, lanes), lanes)
                summed = dot(one, ys[j, :, :, at_n].reshape(2 * cap, lanes))
                part[d, 4 * g + j, :, at_n] = summed.astype(BF16)

    def compute_f(g):
        select(0, g)
        dispatch(0, g)
        for m in range(2):
            @pl.loop(0, 2 * units // 256)
            def _(n):
                at_n = pl.ds(pl.multiple_of(n * 256, 256), 256)
                act[:, at_n] = dot(xs[:, m].reshape(4 * cap, width), wgu[m, :, at_n])

            gate = act[:, 0:units]
            hid[:, 0:units] = (gate / (1.0 + jnp.exp(-gate)) * act[:, units : 2 * units]).astype(BF16)

            @pl.loop(0, width // lanes)
            def _(n):
                at_n = pl.ds(pl.multiple_of(n * lanes, lanes), lanes)
                made = dot(hid[:, 0:units], wdn[m, :, at_n]).reshape(4, cap, lanes)
                ys[:, m, :, at_n] = (made * sgate[:, m]).astype(BF16)

        collect(0, g)

    def compute_b(g):
        select(1, g)
        dispatch(1, g)
        for m in range(2):
            @pl.loop(0, units // 128)
            def _(n):
                at_n = pl.ds(pl.multiple_of(n * 128, 128), 128)
                act[:, at_n] = dot_t(xs[:, m].reshape(4 * cap, width), wdn[m, at_n, :])

            grad = act[:, 0:units]
            pre = sav[m, 4 * g : 4 * g + 4].reshape(4 * cap, 2 * units)
            p, q = pre[:, 0:units].astype(F32), pre[:, units : 2 * units].astype(F32)
            sigma = 1.0 / (1.0 + jnp.exp(-p))
            hid[:, 0:units] = (grad * q * sigma * (1.0 + p * (1.0 - sigma))).astype(BF16)
            hid[:, units : 2 * units] = (grad * p * sigma).astype(BF16)

            @pl.loop(0, width // lanes)
            def _(n):
                at_n = pl.ds(pl.multiple_of(n * lanes, lanes), lanes)
                made = dot_t(hid[...], wgu[m, at_n, :]).reshape(4, cap, lanes)
                ys[:, m, :, at_n] = made.astype(BF16)

        collect(1, g)

    per_half = half // PIECE
    opps, msgs, rels = {}, {}, {}
    for d in range(2):
        for g in range(2):
            for i in range(per_half):
                r = pl.ds(i * PIECE, PIECE)
                r_high = pl.ds(half + i * PIECE, PIECE)
                opps[d, g, 0, i] = send(part.at[d, 4 * g + 2, r], opp.at[d, g, 0, r], up)
                opps[d, g, 1, i] = send(part.at[d, 4 * g + 2, r_high], opp.at[d, g, 1, r], down)
            for i in range(2 * per_half):
                r = pl.ds(i * PIECE, PIECE)
                msgs[d, g, 0, i] = send(part.at[d, 4 * g + 1, r], near.at[d, g, 0, r], up)
                msgs[d, g, 1, i] = send(part.at[d, 4 * g + 3, r], near.at[d, g, 1, r], down)
                rels[d, g, i] = send(part.at[d, 4 * g, r], rel.at[d, g, r], (nexts, prevs)[d][g])

    def combine_1(d, g):
        for i in range(per_half):
            opps[d, g, 0, i].start()
            opps[d, g, 1, i].start()
        for i in range(per_half):
            msgs[d, g, 0, per_half + i].start()
            msgs[d, g, 1, i].start()

    def combine_2(d, g):
        for i in range(per_half):
            r = pl.ds(i * PIECE, PIECE)
            r_high = pl.ds(half + i * PIECE, PIECE)
            opps[d, g, 0, i].wait_recv()
            part[d, 4 * g + 1, r] = (part[d, 4 * g + 1, r].astype(F32) + opp[d, g, 0, r].astype(F32)).astype(BF16)
            msgs[d, g, 0, i].start()
            opps[d, g, 1, i].wait_recv()
            part[d, 4 * g + 3, r_high] = (part[d, 4 * g + 3, r_high].astype(F32) + opp[d, g, 1, r].astype(F32)).astype(BF16)
            msgs[d, g, 1, per_half + i].start()

    def combine_3(d, g):
        for i in range(2 * per_half):
            r = pl.ds(i * PIECE, PIECE)
            msgs[d, g, 0, i].wait_recv()
            msgs[d, g, 1, i].wait_recv()
            total = part[d, 4 * g, r].astype(F32) + near[d, g, 0, r].astype(F32) + near[d, g, 1, r].astype(F32)
            if g == 0:
                total = total + tok[d, 0, r].astype(F32)
            part[d, 4 * g, r] = total.astype(BF16)
            rels[d, g, i].start()

    def finish(d):
        out = (out_f, out_b)[d]
        for i in range(2 * per_half):
            r = pl.ds(i * PIECE, PIECE)
            rels[d, 0, i].wait_recv()
            rels[d, 1, i].wait_recv()
            out[r, :] = (rel[d, 0, r].astype(F32) + rel[d, 1, r].astype(F32)).astype(BF16)

    tab_z.start()
    for copy in tab_y[0]:
        copy.start()
    own[0, 0, 0, 0].start()
    own[0, 0, 1, 1].start()
    own[0, 0, 0, 1].start()
    own[0, 0, 1, 0].start()
    over[0, 0].start()
    over[0, 1].start()
    for copy in twin_w + twin_s:
        copy.start()
    tab_y[0][0].wait_recv()
    tab_o[0].start()
    tab_z.wait_recv()
    for copy in tab_y[1]:
        copy.start()
    tab_y[1][0].wait_recv()
    tab_o[1].start()
    forward(0, 0)
    own[1, 0, 0, 0].start()
    own[1, 0, 1, 1].start()
    own[1, 0, 0, 1].start()
    own[1, 0, 1, 0].start()
    over[0, 0].wait_recv()
    over[1, 0].start()
    start_own(0, 1, 0)
    for copy in load_tok + load_w + load_s:
        copy.wait()
    for copy in twin_w + twin_s:
        copy.wait_recv()
    for copy in [tab_y[0][1], tab_y[1][1]] + tab_o:
        copy.wait_recv()
    complete(0, 0)
    compute_f(0)
    forward(1, 0)
    over[0, 1].wait_recv()
    over[1, 1].start()
    start_own(0, 1, 1)
    complete(1, 0)
    compute_b(0)
    forward(0, 1)
    over[1, 0].wait_recv()
    start_own(1, 1, 0)
    over[1, 1].wait_recv()
    start_own(1, 1, 1)
    complete(0, 1)
    compute_f(1)
    combine_1(0, 1)
    forward(1, 1)
    complete(1, 1)
    compute_b(1)
    combine_1(1, 1)
    combine_2(0, 1)
    combine_1(0, 0)
    combine_2(1, 1)
    combine_3(0, 1)
    combine_1(1, 0)
    combine_2(0, 0)
    combine_3(1, 1)
    combine_2(1, 0)
    combine_3(0, 0)
    combine_3(1, 0)
    finish(0)
    finish(1)
    for copy in remote:
        copy.wait_send()


def shards(
    fwd_tokens, fwd_experts, fwd_gates, gate_proj, up_proj, down_proj, bwd_grads, bwd_experts, bwd_gates, saved_pre
):
    rows, width = fwd_tokens.shape[1:]
    units = gate_proj.shape[3]
    cap = saved_pre.shape[3]
    table = jnp.concatenate(
        [fwd_experts[0].T.astype(F32), fwd_gates[0].T, bwd_experts[0].T.astype(F32), bwd_gates[0].T], axis=0
    )
    hbm = pl.BlockSpec(memory_space=pl.ANY)
    vmem = pl.BlockSpec(memory_space=pltpu.VMEM)
    copies = 128
    out = jax.ShapeDtypeStruct((rows, width), BF16)
    out_f, out_b = pl.pallas_call(
        body,
        out_shape=(out, out),
        in_specs=[vmem] + [hbm] * 6,
        out_specs=(vmem, vmem),
        scratch_shapes=[
            pltpu.VMEM((2, 8, rows, width), BF16),
            pltpu.VMEM((8, 32, rows), F32),
            pltpu.VMEM((2, width, 2 * units), BF16),
            pltpu.VMEM((2, units, width), BF16),
            pltpu.VMEM((2, 8, cap, 2 * units), BF16),
            pltpu.VMEM((4, 2, cap, width), BF16),
            pltpu.VMEM((4, 2, cap, width), BF16),
            pltpu.VMEM((4 * cap, 2 * units), F32),
            pltpu.VMEM((4 * cap, 2 * units), BF16),
            pltpu.VMEM((4, 2 * cap, rows), F32),
            pltpu.VMEM((4, rows, 2 * cap), BF16),
            pltpu.VMEM((4, 2, cap, 1), F32),
            pltpu.VMEM((16, rows), F32),
            pltpu.VMEM((2, 8, rows, width), BF16),
            pltpu.VMEM((2, 2, 2, rows // 2, width), BF16),
            pltpu.VMEM((2, 2, 2, rows, width), BF16),
            pltpu.VMEM((2, 2, rows, width), BF16),
            pltpu.SemaphoreType.DMA((copies,)),
            pltpu.SemaphoreType.DMA((copies,)),
            pltpu.SemaphoreType.DMA((16,)),
        ],
        compiler_params=pltpu.CompilerParams(
            collective_id=0, has_side_effects=True, vmem_limit_bytes=60 * 1024 * 1024
        ),
        cost_estimate=pl.CostEstimate(flops=16 * 10**9, bytes_accessed=12 * 10**6, transcendentals=10**6),
    )(
        table, fwd_tokens[0], bwd_grads[0], gate_proj[0, 0], up_proj[0, 0], down_proj[0, 0], saved_pre[0, :, 0]
    )
    return out_f[None], out_b[None]


def solution(mesh):
    rows = P("section", "expert", None)
    weights = P("section", "expert", None, None)
    placed = (rows, rows, rows, weights, weights, weights, rows, rows, rows, P("section", None, "expert", None, None))
    return jax.shard_map(shards, mesh=mesh, in_specs=placed, out_specs=(rows, rows), check_vma=False)
```

time: 592 us -> 200 us (0.34); the launches traced: 580 us -> 197 us
  waiting for transfers between devices: 424 us -> 0 us
  Pallas kernels: 0 us -> 191 us
  local copies, waits for them, and re-layouts: 76.7 us -> 3.76 us
  matrix products: 30.4 us -> 0 us
  starting transfers between devices: 23.5 us -> 0 us
  other arithmetic: 24.1 us -> 2.02 us
    all_to_all x4 -> x0, waiting for transfers between devices: 411 us -> none  [the longest x1 108 us: shards(): lax.all_to_all(fwd_buffer, 'expert', split_axis=0, concat_axis=0, tiled=T...]
    pallas_call x0 -> x1, Pallas kernels: none -> 191 us  [shards(): pl.pallas_call(body, out_shape=(out, out), in_specs=[vmem] + [hbm] * 6, o...]
    gather x11 -> x0, local copies, waits for them, and re-layouts: 55.7 us -> none  [the longest x6 14.5 us: slot_tables(): place = jnp.take_along_axis(ahead, expert_ids, axis=1)]
    dot_general x5 -> x0, matrix products: 30.4 us -> none  [the longest x1 9.85 us: shards(): jnp.einsum('nscf,sfd->nscd', hidden, w_down, preferred_element_type=jnp.f...]
    all_to_all x4 -> x0, starting transfers between devices: 23.3 us -> none  [the longest x1 9.16 us: shards(): lax.all_to_all(bwd_buffer, 'expert', split_axis=0, concat_axis=0, tiled=T...]
    scatter x4 -> x0, local copies, waits for them, and re-layouts: 17.3 us -> none  [the longest x2 8.68 us: slot_tables(): jnp.zeros((experts_all * capacity,), jnp.bool_).at[flat_rows].set(True)]
    ppermute x2 -> x0, waiting for transfers between devices: 13.2 us -> none  [from_behind(): lax.ppermute(shard, axis, [(i, (i + by) % count) for i in range(count)])]
    reduce_sum x4 -> x0, other arithmetic: 12.3 us -> none  [the longest x1 6.53 us: shards(): jnp.sum(fwd_gates[0][:, :, None] * fwd_picked.astype(jnp.float32), axis=1)]
  transfers between devices with their start and end apart: 6 -> 0, of which waited for: 5 -> 0; matrix products, arithmetic and copies ran while one was open for 16% -> 0% of each run, Pallas kernels for 0% -> 0%
where the time goes in v1:
time: 200 us; the launch traced here: 197 us
  Pallas kernels  191 us (96%)
  local copies, waits for them, and re-layouts  3.76 us (2%)
  other arithmetic  2.02 us (1%)
    pallas_call x1, Pallas kernels, shards(): pl.pallas_call(body, out_shape=(out, out), in_specs=[vmem] + [hbm] * 6, o...  191 us

profile of v1, /device:TPU:96, one launch (start us, length us, event | category | flops | bytes accessed | tf_op | source)
XLA Modules:
  0.0 197.0 jit_solution(4576573010714448865)
XLA Ops:
  0.6 0.7 convert_bitcast_fusion
  1.3 1.3 pad_maximum_fusion.tab_in
  2.6 190.6 %shard_map.113 = (bf16[128,2048]{1,0:T(8,128)(2,1)}, bf16[128,2048]{1,0:T(8,128)(2,1)}) custom-call(f32[32,128]{1,0:T(8,128)} %pad_maximum_fusion.tab_in, bf16[128,2048]{1,0:T(8,128)(2,1)} %bitcast.30, bf16[128,2048]{1,0:T(8,128)(2,1)} %bitcast.31, bf16[2048,384]{1,0:T(8,128)(2,1)} %bitcast.27, bf16[2048,384]{1,0:T(8,128)(2,1)} %bitcast.28, ...), custom_call_target="tpu_custom_call" | custom-call | flops 16000000000 | bytes 12000000 | tf_op jit(solution)/shard_map/pallas_call | solution.py:352
  193.3 1.9 copy.14
  195.2 1.9 copy.15

commit v2 on v1

--- a/solution.py
+++ b/solution.py
@@ -6,7 +6,7 @@
 from jax.sharding import PartitionSpec as P
 
 Y_SIZE, HALVES, CORES = 4, 2, 2
-PIECE = 32
+PIECES = tuple((16 * k, 16) for k in range(4))
 MESH = pl.DeviceIdType.MESH
 F32, BF16 = jnp.float32, jnp.bfloat16
 
@@ -20,8 +20,8 @@
 
 
 def body(
-    tab_in, xf, xb, wg, wu, wd, saved, out_f, out_b,
-    tok, tab, wgu, wdn, sav, xs, ys, act, hid, sel, sel_t, sgate, chosen, part, opp, near, rel,
+    fe, fg, be, bg, xf, xb, wg, wu, wd, saved, rel_f, rel_b,
+    tok, tab, wgu, wdn, sav, xs, ys, act, hid, sel, sel_t, sgate, chosen, part, opp, near,
     dma_send, dma_recv, dma_local,
 ):
     section, expert = lax.axis_index("section"), lax.axis_index("expert")
@@ -31,7 +31,6 @@
     units = wg.shape[1]
     cap = saved.shape[1]
     half = rows // 2
-    lanes = 512
 
     def at(dy, dh=0, dc=0, ds=0):
         return (
@@ -81,7 +80,10 @@
     load_s = [local(saved.at[block_of(j, c)], sav.at[0, j]) for j in range(8)]
     for copy in load_tok + load_w + load_s:
         copy.start()
-    tab[0] = tab_in[...]
+    tab[0, 0:8, :] = fe[...].astype(F32)
+    tab[0, 8:16, :] = fg[...]
+    tab[0, 16:24, :] = be[...].astype(F32)
+    tab[0, 24:32, :] = bg[...]
     pl.semaphore_wait(barrier, len(greeted))
 
     low, high = pl.ds(0, half), pl.ds(half, half)
@@ -151,122 +153,77 @@
 
     def dispatch(d, g):
         for j in range(4):
-            one = sel[j].astype(BF16)
-
-            @pl.loop(0, width // lanes)
-            def _(n):
-                at_n = pl.ds(pl.multiple_of(n * lanes, lanes), lanes)
-                moved = dot(one, tok[d, 4 * g + j, :, at_n]).reshape(2, cap, lanes)
-                if d == 1:
-                    moved = moved * sgate[j]
-                xs[j, :, :, at_n] = moved.astype(BF16)
+            moved = dot(sel[j].astype(BF16), tok[d, 4 * g + j]).reshape(2, cap, width)
+            if d == 1:
+                moved = moved * sgate[j]
+            xs[j] = moved.astype(BF16)
 
     def collect(d, g):
         for j in range(4):
-            one = sel_t[j]
-
-            @pl.loop(0, width // lanes)
-            def _(n):
-                at_n = pl.ds(pl.multiple_of(n * lanes, lanes), lanes)
-                summed = dot(one, ys[j, :, :, at_n].reshape(2 * cap, lanes))
-                part[d, 4 * g + j, :, at_n] = summed.astype(BF16)
+            part[d, 4 * g + j] = dot(sel_t[j], ys[j].reshape(2 * cap, width)).astype(BF16)
 
     def compute_f(g):
         select(0, g)
         dispatch(0, g)
         for m in range(2):
-            @pl.loop(0, 2 * units // 256)
-            def _(n):
-                at_n = pl.ds(pl.multiple_of(n * 256, 256), 256)
-                act[:, at_n] = dot(xs[:, m].reshape(4 * cap, width), wgu[m, :, at_n])
-
+            act[...] = dot(xs[:, m].reshape(4 * cap, width), wgu[m])
             gate = act[:, 0:units]
             hid[:, 0:units] = (gate / (1.0 + jnp.exp(-gate)) * act[:, units : 2 * units]).astype(BF16)
-
-            @pl.loop(0, width // lanes)
-            def _(n):
-                at_n = pl.ds(pl.multiple_of(n * lanes, lanes), lanes)
-                made = dot(hid[:, 0:units], wdn[m, :, at_n]).reshape(4, cap, lanes)
-                ys[:, m, :, at_n] = (made * sgate[:, m]).astype(BF16)
-
+            made = dot(hid[:, 0:units], wdn[m]).reshape(4, cap, width)
+            ys[:, m] = (made * sgate[:, m]).astype(BF16)
         collect(0, g)
 
     def compute_b(g):
         select(1, g)
         dispatch(1, g)
         for m in range(2):
-            @pl.loop(0, units // 128)
-            def _(n):
-                at_n = pl.ds(pl.multiple_of(n * 128, 128), 128)
-                act[:, at_n] = dot_t(xs[:, m].reshape(4 * cap, width), wdn[m, at_n, :])
-
+            act[:, 0:units] = dot_t(xs[:, m].reshape(4 * cap, width), wdn[m])
             grad = act[:, 0:units]
             pre = sav[m, 4 * g : 4 * g + 4].reshape(4 * cap, 2 * units)
             p, q = pre[:, 0:units].astype(F32), pre[:, units : 2 * units].astype(F32)
             sigma = 1.0 / (1.0 + jnp.exp(-p))
             hid[:, 0:units] = (grad * q * sigma * (1.0 + p * (1.0 - sigma))).astype(BF16)
             hid[:, units : 2 * units] = (grad * p * sigma).astype(BF16)
-
-            @pl.loop(0, width // lanes)
-            def _(n):
-                at_n = pl.ds(pl.multiple_of(n * lanes, lanes), lanes)
-                made = dot_t(hid[...], wgu[m, at_n, :]).reshape(4, cap, lanes)
-                ys[:, m, :, at_n] = made.astype(BF16)
-
+            ys[:, m] = dot_t(hid[...], wgu[m]).reshape(4, cap, width).astype(BF16)
         collect(1, g)
 
-    per_half = half // PIECE
-    opps, msgs, rels = {}, {}, {}
+    rels = (rel_f, rel_b)
+    opps, msgs, outs = {}, {}, {}
+    pieces = {}
     for d in range(2):
         for g in range(2):
-            for i in range(per_half):
-                r = pl.ds(i * PIECE, PIECE)
-                r_high = pl.ds(half + i * PIECE, PIECE)
-                opps[d, g, 0, i] = send(part.at[d, 4 * g + 2, r], opp.at[d, g, 0, r], up)
-                opps[d, g, 1, i] = send(part.at[d, 4 * g + 2, r_high], opp.at[d, g, 1, r], down)
-            for i in range(2 * per_half):
-                r = pl.ds(i * PIECE, PIECE)
-                msgs[d, g, 0, i] = send(part.at[d, 4 * g + 1, r], near.at[d, g, 0, r], up)
-                msgs[d, g, 1, i] = send(part.at[d, 4 * g + 3, r], near.at[d, g, 1, r], down)
-                rels[d, g, i] = send(part.at[d, 4 * g, r], rel.at[d, g, r], (nexts, prevs)[d][g])
-
-    def combine_1(d, g):
-        for i in range(per_half):
-            opps[d, g, 0, i].start()
-            opps[d, g, 1, i].start()
-        for i in range(per_half):
-            msgs[d, g, 0, per_half + i].start()
-            msgs[d, g, 1, i].start()
-
-    def combine_2(d, g):
-        for i in range(per_half):
-            r = pl.ds(i * PIECE, PIECE)
-            r_high = pl.ds(half + i * PIECE, PIECE)
-            opps[d, g, 0, i].wait_recv()
-            part[d, 4 * g + 1, r] = (part[d, 4 * g + 1, r].astype(F32) + opp[d, g, 0, r].astype(F32)).astype(BF16)
-            msgs[d, g, 0, i].start()
-            opps[d, g, 1, i].wait_recv()
-            part[d, 4 * g + 3, r_high] = (part[d, 4 * g + 3, r_high].astype(F32) + opp[d, g, 1, r].astype(F32)).astype(BF16)
-            msgs[d, g, 1, per_half + i].start()
-
-    def combine_3(d, g):
-        for i in range(2 * per_half):
-            r = pl.ds(i * PIECE, PIECE)
-            msgs[d, g, 0, i].wait_recv()
-            msgs[d, g, 1, i].wait_recv()
+            for k, (first, size) in enumerate(PIECES):
+                lo, hi = pl.ds(first, size), pl.ds(half + first, size)
+                pieces[g, k] = (lo, hi)
+                opps[d, g, k, 0] = send(part.at[d, 4 * g + 2, lo], opp.at[d, g, 0, lo], up)
+                opps[d, g, k, 1] = send(part.at[d, 4 * g + 2, hi], opp.at[d, g, 1, lo], down)
+                for i, r in enumerate((lo, hi)):
+                    msgs[d, g, k, 0, i] = send(part.at[d, 4 * g + 1, r], near.at[d, g, 0, r], up)
+                    msgs[d, g, k, 1, i] = send(part.at[d, 4 * g + 3, r], near.at[d, g, 1, r], down)
+                    outs[d, g, k, i] = send(part.at[d, 4 * g, r], rels[d].at[g, r], (nexts, prevs)[d][g])
+
+    def begin(d, g, k):
+        opps[d, g, k, 0].start()
+        opps[d, g, k, 1].start()
+        msgs[d, g, k, 0, 1].start()
+        msgs[d, g, k, 1, 0].start()
+
+    def add_on(d, g, k):
+        lo, hi = pieces[g, k]
+        for i, (r, j) in enumerate(((lo, 1), (hi, 3))):
+            opps[d, g, k, i].wait_recv()
+            part[d, 4 * g + j, r] = (part[d, 4 * g + j, r].astype(F32) + opp[d, g, i, lo].astype(F32)).astype(BF16)
+            msgs[d, g, k, i, i].start()
+
+    def relay(d, g, k):
+        for i, r in enumerate(pieces[g, k]):
+            msgs[d, g, k, 0, i].wait_recv()
+            msgs[d, g, k, 1, i].wait_recv()
             total = part[d, 4 * g, r].astype(F32) + near[d, g, 0, r].astype(F32) + near[d, g, 1, r].astype(F32)
             if g == 0:
                 total = total + tok[d, 0, r].astype(F32)
             part[d, 4 * g, r] = total.astype(BF16)
-            rels[d, g, i].start()
-
-    def finish(d):
-        out = (out_f, out_b)[d]
-        for i in range(2 * per_half):
-            r = pl.ds(i * PIECE, PIECE)
-            rels[d, 0, i].wait_recv()
-            rels[d, 1, i].wait_recv()
-            out[r, :] = (rel[d, 0, r].astype(F32) + rel[d, 1, r].astype(F32)).astype(BF16)
+            outs[d, g, k, i].start()
 
     tab_z.start()
     for copy in tab_y[0]:
@@ -315,23 +272,21 @@
     start_own(1, 1, 1)
     complete(0, 1)
     compute_f(1)
-    combine_1(0, 1)
-    forward(1, 1)
-    complete(1, 1)
-    compute_b(1)
-    combine_1(1, 1)
-    combine_2(0, 1)
-    combine_1(0, 0)
-    combine_2(1, 1)
-    combine_3(0, 1)
-    combine_1(1, 0)
-    combine_2(0, 0)
-    combine_3(1, 1)
-    combine_2(1, 0)
-    combine_3(0, 0)
-    combine_3(1, 0)
-    finish(0)
-    finish(1)
+    jobs = [(0, 1, 0), (0, 1, 1), (1, 1, 0), (1, 1, 1), (1, 1, 2), (0, 1, 2), (1, 1, 3), (0, 1, 3)]
+    jobs += [(d, 0, k) for k in range(len(PIECES)) for d in range(2)]
+    for i in range(len(jobs) + 4):
+        if i == 2:
+            forward(1, 1)
+            complete(1, 1)
+            compute_b(1)
+        if i < len(jobs):
+            begin(*jobs[i])
+        if 2 <= i < len(jobs) + 2:
+            add_on(*jobs[i - 2])
+        if i >= 4:
+            relay(*jobs[i - 4])
+    for copy in outs.values():
+        copy.wait_recv()
     for copy in remote:
         copy.wait_send()
 
@@ -342,18 +297,15 @@
     rows, width = fwd_tokens.shape[1:]
     units = gate_proj.shape[3]
     cap = saved_pre.shape[3]
-    table = jnp.concatenate(
-        [fwd_experts[0].T.astype(F32), fwd_gates[0].T, bwd_experts[0].T.astype(F32), bwd_gates[0].T], axis=0
-    )
     hbm = pl.BlockSpec(memory_space=pl.ANY)
     vmem = pl.BlockSpec(memory_space=pltpu.VMEM)
-    copies = 128
-    out = jax.ShapeDtypeStruct((rows, width), BF16)
-    out_f, out_b = pl.pallas_call(
+    copies = 256
+    out = jax.ShapeDtypeStruct((2, rows, width), BF16)
+    rel_f, rel_b = pl.pallas_call(
         body,
         out_shape=(out, out),
-        in_specs=[vmem] + [hbm] * 6,
-        out_specs=(vmem, vmem),
+        in_specs=[vmem] * 4 + [hbm] * 6,
+        out_specs=(hbm, hbm),
         scratch_shapes=[
             pltpu.VMEM((2, 8, rows, width), BF16),
             pltpu.VMEM((8, 32, rows), F32),
@@ -371,7 +323,6 @@
             pltpu.VMEM((2, 8, rows, width), BF16),
             pltpu.VMEM((2, 2, 2, rows // 2, width), BF16),
             pltpu.VMEM((2, 2, 2, rows, width), BF16),
-            pltpu.VMEM((2, 2, rows, width), BF16),
             pltpu.SemaphoreType.DMA((copies,)),
             pltpu.SemaphoreType.DMA((copies,)),
             pltpu.SemaphoreType.DMA((16,)),
@@ -381,9 +332,14 @@
         ),
         cost_estimate=pl.CostEstimate(flops=16 * 10**9, bytes_accessed=12 * 10**6, transcendentals=10**6),
     )(
-        table, fwd_tokens[0], bwd_grads[0], gate_proj[0, 0], up_proj[0, 0], down_proj[0, 0], saved_pre[0, :, 0]
+        fwd_experts[0].T, fwd_gates[0].T, bwd_experts[0].T, bwd_gates[0].T, fwd_tokens[0], bwd_grads[0],
+        gate_proj[0, 0], up_proj[0, 0], down_proj[0, 0], saved_pre[0, :, 0],
     )
-    return out_f[None], out_b[None]
+    return both(rel_f), both(rel_b)
+
+
+def both(parts):
+    return (parts[0:1].astype(F32) + parts[1:2].astype(F32)).astype(BF16)
 
 
 def solution(mesh):

time: 200 us -> 169 us (0.84)
  Pallas kernels: 191 us -> 163 us
  local copies, waits for them, and re-layouts: 3.76 us -> 0 us
    pallas_call x1, Pallas kernels: 191 us -> 163 us  [shards(): pl.pallas_call(body, out_shape=(out, out), in_specs=[vmem] * 4 + [hbm] *...]
    unnamed x2 -> x0, local copies, waits for them, and re-layouts: 3.76 us -> none
    convert_element_type x1, other arithmetic: 0.71 us -> 2.88 us  [both(): return (parts[0:1].astype(F32) + parts[1:2].astype(F32)).astype(BF16)]
where the time goes in v2:
time: 169 us; the launch traced here: 166 us
  Pallas kernels  163 us (96%)
  other arithmetic  2.88 us (2%)
    pallas_call x1, Pallas kernels, shards(): pl.pallas_call(body, out_shape=(out, out), in_specs=[vmem] * 4 + [hbm] *...  163 us

profile of v2, /device:TPU:96, one launch (start us, length us, event | category | flops | bytes accessed | tf_op | source)
XLA Modules:
  0.0 166.4 jit_solution(12548639986504657008)
XLA Ops:
  0.6 162.8 %shard_map.113 = (bf16[2,128,2048]{2,1,0:T(8,128)(2,1)}, bf16[2,128,2048]{2,1,0:T(8,128)(2,1)}) custom-call(s32[8,128]{1,0:T(8,128)} %bitcast.24, f32[8,128]{1,0:T(8,128)} %bitcast.25, s32[8,128]{1,0:T(8,128)} %bitcast.26, f32[8,128]{1,0:T(8,128)} %bitcast.27, bf16[128,2048]{1,0:T(8,128)(2,1)} %bitcast.22, bf16[128,2048]{1,0:T(8,128)(2,1)} %bitcast.23, ...), custom_call_target="tpu_custom_call" | custom-call | flops 16000000000 | bytes 12000000 | tf_op jit(solution)/shard_map/pallas_call | solution.py:304
  163.5 2.9 %add_convert_fusion = (bf16[1,128,2048]{2,1,0:T(8,128)(2,1)}, bf16[1,128,2048]{2,1,0:T(8,128)(2,1)}) fusion(bf16[2,128,2048]{2,1,0:T(8,128)(2,1)} %get-tuple-element.5, bf16[2,128,2048]{2,1,0:T(8,128)(2,1)} %get-tuple-element.4), kind=kLoop, calls=%fused_computation | loop fusion | flops 2097152 | bytes 3145728 | tf_op jit(solution)/shard_map/convert_element_type | solution.py:342

commit v3 on v2

--- a/solution.py
+++ b/solution.py
@@ -6,6 +6,7 @@
 from jax.sharding import PartitionSpec as P
 
 Y_SIZE, HALVES, CORES = 4, 2, 2
+LIFT = 16
 PIECES = tuple((16 * k, 16) for k in range(4))
 MESH = pl.DeviceIdType.MESH
 F32, BF16 = jnp.float32, jnp.bfloat16
@@ -21,7 +22,7 @@
 
 def body(
     fe, fg, be, bg, xf, xb, wg, wu, wd, saved, rel_f, rel_b,
-    tok, tab, wgu, wdn, sav, xs, ys, act, hid, sel, sel_t, sgate, chosen, part, opp, near,
+    tok, tab, wgu, wdn, sav, xs, ys, act, hid, sel, sel_t, sgate, chosen, part, opp, near, lift,
     dma_send, dma_recv, dma_local,
 ):
     section, expert = lax.axis_index("section"), lax.axis_index("expert")
@@ -87,6 +88,8 @@
     pl.semaphore_wait(barrier, len(greeted))
 
     low, high = pl.ds(0, half), pl.ds(half, half)
+    rest_low, rest_high = pl.ds(LIFT, half - LIFT), pl.ds(half + LIFT, half - LIFT)
+    lifted = (pl.ds(0, LIFT), pl.ds(half, LIFT))
     tab_z = send(tab.at[0], tab.at[4], across)
     tab_y = [(send(tab.at[4 * g], tab.at[4 * g + 3], up), send(tab.at[4 * g], tab.at[4 * g + 1], down)) for g in range(2)]
     tab_o = [send(tab.at[4 * g + 3], tab.at[4 * g + 2], up) for g in range(2)]
@@ -101,11 +104,13 @@
         for i, r in enumerate((low, high)):
             over[d, i] = send(inputs[d].at[r], tok.at[d, 4, r], across)
         for g in range(2):
-            for i, r in enumerate((low, high)):
+            halves = (low, high) if (d, g) != (1, 1) else (rest_low, rest_high)
+            for i, r in enumerate(halves):
                 own[d, g, 0, i] = send(source(d, g, r), tok.at[d, 4 * g + 3, r], up)
                 own[d, g, 1, i] = send(source(d, g, r), tok.at[d, 4 * g + 1, r], down)
-            fwd[d, g, 0] = send(tok.at[d, 4 * g + 3, low], tok.at[d, 4 * g + 2, low], up)
-            fwd[d, g, 1] = send(tok.at[d, 4 * g + 1, high], tok.at[d, 4 * g + 2, high], down)
+            fwd[d, g, 0] = send(tok.at[d, 4 * g + 3, halves[0]], tok.at[d, 4 * g + 2, halves[0]], up)
+            fwd[d, g, 1] = send(tok.at[d, 4 * g + 1, halves[1]], tok.at[d, 4 * g + 2, halves[1]], down)
+    cross = [send(tok.at[1, j, r], tok.at[1, 4 + j, r], across) for j in range(1, 4) for r in lifted]
     twin_w = [
         send(wg, wgu.at[1, :, pl.ds(0, units)], twin),
         send(wu, wgu.at[1, :, pl.ds(units, units)], twin),
@@ -195,12 +200,21 @@
             for k, (first, size) in enumerate(PIECES):
                 lo, hi = pl.ds(first, size), pl.ds(half + first, size)
                 pieces[g, k] = (lo, hi)
+                for i, r in enumerate((lo, hi)):
+                    outs[d, g, k, i] = send(part.at[d, 4 * g, r], rels[d].at[g, r], (nexts, prevs)[d][g])
+                if (d, g, k) == (0, 1, 0):
+                    continue
                 opps[d, g, k, 0] = send(part.at[d, 4 * g + 2, lo], opp.at[d, g, 0, lo], up)
                 opps[d, g, k, 1] = send(part.at[d, 4 * g + 2, hi], opp.at[d, g, 1, lo], down)
                 for i, r in enumerate((lo, hi)):
                     msgs[d, g, k, 0, i] = send(part.at[d, 4 * g + 1, r], near.at[d, g, 0, r], up)
                     msgs[d, g, k, 1, i] = send(part.at[d, 4 * g + 3, r], near.at[d, g, 1, r], down)
-                    outs[d, g, k, i] = send(part.at[d, 4 * g, r], rels[d].at[g, r], (nexts, prevs)[d][g])
+    lifts = {(j, i): send(part.at[0, 4 + j, r], lift.at[j - 1, i], across) for j in range(1, 4) for i, r in enumerate(lifted)}
+
+    def take_lifts():
+        for (j, i), copy in lifts.items():
+            copy.wait_recv()
+            part[0, j, lifted[i]] = (part[0, j, lifted[i]].astype(F32) + lift[j - 1, i].astype(F32)).astype(BF16)
 
     def begin(d, g, k):
         opps[d, g, k, 0].start()
@@ -264,6 +278,8 @@
     over[1, 1].start()
     start_own(0, 1, 1)
     complete(1, 0)
+    for copy in cross:
+        copy.start()
     compute_b(0)
     forward(0, 1)
     over[1, 0].wait_recv()
@@ -272,19 +288,39 @@
     start_own(1, 1, 1)
     complete(0, 1)
     compute_f(1)
-    jobs = [(0, 1, 0), (0, 1, 1), (1, 1, 0), (1, 1, 1), (1, 1, 2), (0, 1, 2), (1, 1, 3), (0, 1, 3)]
-    jobs += [(d, 0, k) for k in range(len(PIECES)) for d in range(2)]
-    for i in range(len(jobs) + 4):
-        if i == 2:
-            forward(1, 1)
-            complete(1, 1)
-            compute_b(1)
-        if i < len(jobs):
-            begin(*jobs[i])
-        if 2 <= i < len(jobs) + 2:
-            add_on(*jobs[i - 2])
-        if i >= 4:
-            relay(*jobs[i - 4])
+    outs[0, 1, 0, 0].start()
+    outs[0, 1, 0, 1].start()
+    for copy in lifts.values():
+        copy.start()
+    begin(0, 1, 1)
+    forward(1, 1)
+    complete(1, 1)
+    begin(0, 1, 2)
+    for copy in cross:
+        copy.wait_recv()
+    add_on(0, 1, 1)
+    compute_b(1)
+    steps = {"B": begin, "A": add_on, "R": relay}
+    for step in (
+        "B110 B111 A012 B013",
+        "A110 R011 A111 B112",
+        "R110 R012 A013 B113",
+        "A112 R111 B000 A113",
+        "R013 R112 B100 A000",
+        "R113 B001 A100",
+        "B101 A001 R000",
+        "B002 A101 R100",
+        "B102 A002 R001",
+        "B003 A102 R101",
+        "B103 A003 R002",
+        "A103 R102",
+        "R003 R103",
+    ):
+        for name in step.split():
+            d, g, k = (int(x) for x in name[1:])
+            if name == "B000":
+                take_lifts()
+            steps[name[0]](d, g, k)
     for copy in outs.values():
         copy.wait_recv()
     for copy in remote:
@@ -323,6 +359,7 @@
             pltpu.VMEM((2, 8, rows, width), BF16),
             pltpu.VMEM((2, 2, 2, rows // 2, width), BF16),
             pltpu.VMEM((2, 2, 2, rows, width), BF16),
+            pltpu.VMEM((3, 2, LIFT, width), BF16),
             pltpu.SemaphoreType.DMA((copies,)),
             pltpu.SemaphoreType.DMA((copies,)),
             pltpu.SemaphoreType.DMA((16,)),

time: 169 us -> 161 us (0.953); the launches traced: 166 us -> 160 us
  Pallas kernels: 163 us -> 157 us
    pallas_call x1, Pallas kernels: 163 us -> 157 us  [shards(): pl.pallas_call(body, out_shape=(out, out), in_specs=[vmem] * 4 + [hbm] *...]
where the time goes in v3:
time: 161 us; the launch traced here: 160 us
  Pallas kernels  157 us (98%)
  other arithmetic  2.88 us (2%)
    pallas_call x1, Pallas kernels, shards(): pl.pallas_call(body, out_shape=(out, out), in_specs=[vmem] * 4 + [hbm] *...  157 us

profile of v3, /device:TPU:96, one launch (start us, length us, event | category | flops | bytes accessed | tf_op | source)
XLA Modules:
  0.0 160.5 jit_solution(6821052646960336128)
XLA Ops:
  0.6 157.0 %shard_map.113 = (bf16[2,128,2048]{2,1,0:T(8,128)(2,1)}, bf16[2,128,2048]{2,1,0:T(8,128)(2,1)}) custom-call(s32[8,128]{1,0:T(8,128)} %bitcast.24, f32[8,128]{1,0:T(8,128)} %bitcast.25, s32[8,128]{1,0:T(8,128)} %bitcast.26, f32[8,128]{1,0:T(8,128)} %bitcast.27, bf16[128,2048]{1,0:T(8,128)(2,1)} %bitcast.22, bf16[128,2048]{1,0:T(8,128)(2,1)} %bitcast.23, ...), custom_call_target="tpu_custom_call" | custom-call | flops 16000000000 | bytes 12000000 | tf_op jit(solution)/shard_map/pallas_call | solution.py:340
  157.6 2.9 %add_convert_fusion = (bf16[1,128,2048]{2,1,0:T(8,128)(2,1)}, bf16[1,128,2048]{2,1,0:T(8,128)(2,1)}) fusion(bf16[2,128,2048]{2,1,0:T(8,128)(2,1)} %get-tuple-element.5, bf16[2,128,2048]{2,1,0:T(8,128)(2,1)} %get-tuple-element.4), kind=kLoop, calls=%fused_computation | loop fusion | flops 2097152 | bytes 3145728 | tf_op jit(solution)/shard_map/convert_element_type | solution.py:379

commit v4 on v3

--- a/solution.py
+++ b/solution.py
@@ -7,7 +7,10 @@
 
 Y_SIZE, HALVES, CORES = 4, 2, 2
 LIFT = 16
-PIECES = tuple((16 * k, 16) for k in range(4))
+PIECES = (
+    tuple((16 * k, 16, 0, 2) for k in range(3)) + ((48, 16, 0, 1), (48, 16, 1, 1)),
+    tuple((16 * k, 16, 0, 2) for k in range(4)),
+)
 MESH = pl.DeviceIdType.MESH
 F32, BF16 = jnp.float32, jnp.bfloat16
 
@@ -197,18 +200,19 @@
     pieces = {}
     for d in range(2):
         for g in range(2):
-            for k, (first, size) in enumerate(PIECES):
+            for k, (first, size, side, sides) in enumerate(PIECES[g]):
                 lo, hi = pl.ds(first, size), pl.ds(half + first, size)
-                pieces[g, k] = (lo, hi)
+                cols = pl.ds(side * (width // 2), sides * (width // 2))
+                pieces[g, k] = (lo, hi, cols)
                 for i, r in enumerate((lo, hi)):
-                    outs[d, g, k, i] = send(part.at[d, 4 * g, r], rels[d].at[g, r], (nexts, prevs)[d][g])
+                    outs[d, g, k, i] = send(part.at[d, 4 * g, r, cols], rels[d].at[g, r, cols], (nexts, prevs)[d][g])
                 if (d, g, k) == (0, 1, 0):
                     continue
-                opps[d, g, k, 0] = send(part.at[d, 4 * g + 2, lo], opp.at[d, g, 0, lo], up)
-                opps[d, g, k, 1] = send(part.at[d, 4 * g + 2, hi], opp.at[d, g, 1, lo], down)
+                opps[d, g, k, 0] = send(part.at[d, 4 * g + 2, lo, cols], opp.at[d, g, 0, lo, cols], up)
+                opps[d, g, k, 1] = send(part.at[d, 4 * g + 2, hi, cols], opp.at[d, g, 1, lo, cols], down)
                 for i, r in enumerate((lo, hi)):
-                    msgs[d, g, k, 0, i] = send(part.at[d, 4 * g + 1, r], near.at[d, g, 0, r], up)
-                    msgs[d, g, k, 1, i] = send(part.at[d, 4 * g + 3, r], near.at[d, g, 1, r], down)
+                    msgs[d, g, k, 0, i] = send(part.at[d, 4 * g + 1, r, cols], near.at[d, g, 0, r, cols], up)
+                    msgs[d, g, k, 1, i] = send(part.at[d, 4 * g + 3, r, cols], near.at[d, g, 1, r, cols], down)
     lifts = {(j, i): send(part.at[0, 4 + j, r], lift.at[j - 1, i], across) for j in range(1, 4) for i, r in enumerate(lifted)}
 
     def take_lifts():
@@ -223,20 +227,27 @@
         msgs[d, g, k, 1, 0].start()
 
     def add_on(d, g, k):
-        lo, hi = pieces[g, k]
+        lo, hi, cols = pieces[g, k]
         for i, (r, j) in enumerate(((lo, 1), (hi, 3))):
             opps[d, g, k, i].wait_recv()
-            part[d, 4 * g + j, r] = (part[d, 4 * g + j, r].astype(F32) + opp[d, g, i, lo].astype(F32)).astype(BF16)
+            part[d, 4 * g + j, r, cols] = (
+                part[d, 4 * g + j, r, cols].astype(F32) + opp[d, g, i, lo, cols].astype(F32)
+            ).astype(BF16)
             msgs[d, g, k, i, i].start()
 
     def relay(d, g, k):
-        for i, r in enumerate(pieces[g, k]):
+        cols = pieces[g, k][2]
+        for i, r in enumerate(pieces[g, k][:2]):
             msgs[d, g, k, 0, i].wait_recv()
             msgs[d, g, k, 1, i].wait_recv()
-            total = part[d, 4 * g, r].astype(F32) + near[d, g, 0, r].astype(F32) + near[d, g, 1, r].astype(F32)
+            total = (
+                part[d, 4 * g, r, cols].astype(F32)
+                + near[d, g, 0, r, cols].astype(F32)
+                + near[d, g, 1, r, cols].astype(F32)
+            )
             if g == 0:
-                total = total + tok[d, 0, r].astype(F32)
-            part[d, 4 * g, r] = total.astype(BF16)
+                total = total + tok[d, 0, r, cols].astype(F32)
+            part[d, 4 * g, r, cols] = total.astype(BF16)
             outs[d, g, k, i].start()
 
     tab_z.start()
@@ -313,8 +324,10 @@
         "B102 A002 R001",
         "B003 A102 R101",
         "B103 A003 R002",
-        "A103 R102",
-        "R003 R103",
+        "B004 A103 R102",
+        "B104 A004 R003",
+        "A104 R103",
+        "R004 R104",
     ):
         for name in step.split():
             d, g, k = (int(x) for x in name[1:])

time: 161 us -> 161 us (level)
  no operation moved by 1% of the time
where the time goes in v4:
time: 161 us
  Pallas kernels  157 us (98%)
  other arithmetic  2.88 us (2%)
    pallas_call x1, Pallas kernels, shards(): pl.pallas_call(body, out_shape=(out, out), in_specs=[vmem] * 4 + [hbm] *...  157 us

profile of v4, /device:TPU:96, one launch (start us, length us, event | category | flops | bytes accessed | tf_op | source)
XLA Modules:
  0.0 160.6 jit_solution(18282126834853142099)
XLA Ops:
  0.6 157.0 %shard_map.113 = (bf16[2,128,2048]{2,1,0:T(8,128)(2,1)}, bf16[2,128,2048]{2,1,0:T(8,128)(2,1)}) custom-call(s32[8,128]{1,0:T(8,128)} %bitcast.24, f32[8,128]{1,0:T(8,128)} %bitcast.25, s32[8,128]{1,0:T(8,128)} %bitcast.26, f32[8,128]{1,0:T(8,128)} %bitcast.27, bf16[128,2048]{1,0:T(8,128)(2,1)} %bitcast.22, bf16[128,2048]{1,0:T(8,128)(2,1)} %bitcast.23, ...), custom_call_target="tpu_custom_call" | custom-call | flops 16000000000 | bytes 12000000 | tf_op jit(solution)/shard_map/pallas_call | solution.py:353
  157.7 2.9 %add_convert_fusion = (bf16[1,128,2048]{2,1,0:T(8,128)(2,1)}, bf16[1,128,2048]{2,1,0:T(8,128)(2,1)}) fusion(bf16[2,128,2048]{2,1,0:T(8,128)(2,1)} %get-tuple-element.5, bf16[2,128,2048]{2,1,0:T(8,128)(2,1)} %get-tuple-element.4), kind=kLoop, calls=%fused_computation | loop fusion | flops 2097152 | bytes 3145728 | tf_op jit(solution)/shard_map/convert_element_type | solution.py:392
